TPU v7x, 256 devices: a whole 4x4x8 slice. The times are simulated.
256 devices in a mesh: grp: 16 (over x, y), dev: 16 (over z, core).
Axes of the slice: x: 4, y: 4, z: 8, core: 2. Of those that a mesh axis runs over, the one named last changes fastest.
Arguments:
- rows: bfloat16 [2, 32768, 384], P(None, ('grp', 'dev')), may hold values from -6 to 6
- adj_rhs: float32 [2, 32768, 256], P(None, ('grp', 'dev')), may hold values from -6 to 6
- pattern: int32 [32768, 24], P(('grp', 'dev')), may hold values from 0 to 2559
- lengths: int32 [32768], P(('grp', 'dev')), may hold values from 6 to 24, as said below
Outputs:
- applied: float32 [2, 32768, 256], P(None, ('grp', 'dev'))
Inputs may be any that keep to these rules, and one draw needn't show every extreme that they name: `lengths`: every device's first block row uses all 24 entries.
All inputs are finite; a program needn't handle non-finite values.
Results may differ from a plain program's by a relative error of at most 0.0006.
Values may be sent and summed in bfloat16 or wider, within the bound.
A program may use at most 128 MiB of HBM per device.

v0:
```python
import jax
import jax.numpy as jnp
from jax import lax
from jax.sharding import PartitionSpec as P

GHOST = 16


ridge_share = 0.25


def passed_along(block, axis, distance):
    devices = range(lax.axis_size(axis))
    route = [((i - distance) % len(devices), i) for i in devices]
    return lax.ppermute(block, axis, route)


def small_solve(gram, target):
    points, count, slots = target.shape
    matrix = gram.reshape(points * count, slots, slots).transpose(1, 2, 0)
    vector = target.reshape(points * count, slots).transpose(1, 0)
    lower = [[None] * slots for _ in range(slots)]
    for col in range(slots):
        acc = matrix[col, col]
        for mid in range(col):
            acc = acc - lower[col][mid] * lower[col][mid]
        pivot = jnp.sqrt(acc)
        lower[col][col] = pivot
        for below in range(col + 1, slots):
            acc = matrix[below, col]
            for mid in range(col):
                acc = acc - lower[below][mid] * lower[col][mid]
            lower[below][col] = acc / pivot
    forward = []
    for step in range(slots):
        acc = vector[step]
        for mid in range(step):
            acc = acc - lower[step][mid] * forward[mid]
        forward.append(acc / lower[step][step])
    backward = [None] * slots
    for step in range(slots - 1, -1, -1):
        acc = forward[step]
        for mid in range(step + 1, slots):
            acc = acc - lower[mid][step] * backward[mid]
        backward[step] = acc / lower[step][step]
    solved = jnp.stack(backward, axis=0)
    return solved.transpose(1, 0).reshape(points, count, slots)


def weight_table(coeff, where_int, entries):
    slots = where_int.shape[1]
    entry_ids = jnp.arange(entries, dtype=jnp.int32)[:, None]
    table = jnp.zeros((coeff.shape[0], entries, coeff.shape[1]), jnp.float32)
    for slot in range(slots):
        match = where_int[:, slot][None, :] == entry_ids
        table = table + jnp.where(match[None], coeff[:, None, :, slot], 0.0)
    return table


def local(rows, adj_rhs, pattern, lengths):
    points, own_rows, width = rows.shape
    slots = pattern.shape[1]
    ghosts = GHOST
    ext_rows = own_rows + 2 * ghosts
    shared = rows[:, :ghosts]
    from_lower = passed_along(shared, "grp", 1)
    from_upper = passed_along(shared, "grp", -1)
    extended = jnp.concatenate([rows, from_lower, from_upper], axis=1)
    pool = lax.all_gather(extended, "dev", axis=1, tiled=True)
    used = jnp.arange(slots, dtype=jnp.int32)[None, :] < lengths[:, None]
    near = jnp.take(pool, pattern, axis=1)
    near = jnp.where(used[None, :, :, None], near, jnp.zeros((), near.dtype))
    gram = jnp.einsum("prkw,prjw->prkj", near, near, preferred_element_type=jnp.float32)
    gram = gram + ridge_share * width * jnp.eye(slots, dtype=jnp.float32)
    target = jnp.einsum("prkw,prw->prk", near, rows, preferred_element_type=jnp.float32)
    coeff = small_solve(gram, target)
    count = lax.axis_size("dev") * ext_rows
    table = weight_table(coeff, pattern, count)
    partial_sum = jnp.einsum("per,prc->pec", table, adj_rhs, precision=lax.Precision.HIGHEST)
    mine = lax.psum_scatter(partial_sum, "dev", scatter_dimension=1, tiled=True)
    back_lower = passed_along(
        mine[:, own_rows : own_rows + ghosts].astype(jnp.bfloat16), "grp", -1
    ).astype(jnp.float32)
    back_upper = passed_along(mine[:, own_rows + ghosts :], "grp", 1)
    total = mine[:, :own_rows].at[:, :ghosts].add(back_lower + back_upper)
    return adj_rhs - total


def solution(mesh):
    placed = (
        P(None, ("grp", "dev"), None),
        P(None, ("grp", "dev"), None),
        P(("grp", "dev"), None),
        P(("grp", "dev")),
    )
    return jax.shard_map(
        local, mesh=mesh, in_specs=placed, out_specs=P(None, ("grp", "dev"), None), check_vma=False
    )
```

profile of v0, /device:TPU:30, one launch (start us, length us, event | category | flops | bytes accessed | tf_op | source)
XLA Modules:
  0.0 227.1 jit_solution(17447898474967266741)
XLA Ops:
  6.5 1.1 copy.14
  7.7 1.9 collective-permute-start
  9.8 0.7 compare_select_fusion
  10.5 0.7 compare_and_fusion
  11.2 1.0 slice_bitcast_fusion.47
  12.2 1.1 iota_compare_fusion.4
  13.3 1.2 iota_compare_fusion.6
  14.6 0.8 slice_bitcast_fusion.46
  15.4 1.4 collective-permute-done.1
  16.8 1.0 pad_maximum_fusion
  18.4 1.2 iota_compare_fusion.8
  19.6 1.2 iota_compare_fusion.10
  20.8 1.3 iota_compare_fusion.12
  22.1 1.2 iota_compare_fusion.14
  23.3 1.2 iota_compare_fusion.16
  24.5 1.2 iota_compare_fusion.18
  25.7 1.2 iota_compare_fusion.20
  27.0 1.2 iota_compare_fusion.22
  28.2 1.2 iota_compare_fusion
  29.5 1.2 iota_compare_fusion.2
  30.7 30.4 %all-gather.2.cloned.1.call-done = bf16[2,2560,384]{2,0,1:T(2,128)(2,1)} async-done(((bf16[2,160,384]{2,0,1:T(2,128)(2,1)}), bf16[2,2560,384]{2,0,1:T(2,128)(2,1)}) %all-gather.2.cloned.1.call-update) | async-done | bytes 3932176 | tf_op jit(solution)/shard_map/all_gather | solution.py:69
  61.1 30.3 %gather_fusion = bf16[3072,2,384]{2,1,0:T(2,128)(2,1)} fusion(bf16[2,2560,384]{2,0,1:T(2,128)(2,1)} %all-gather.2.cloned.1.call-done, s32[3072]{0:T(1024)S(1)} %broadcast_clamp_fusion), kind=kCustom, calls=%fused_computation | custom fusion | bytes 9449472 | tf_op jit(solution)/shard_map/jit(_take)/gather | solution.py:71
  91.3 8.0 %fusion.59 = f32[2,128,24,24]{3,2,1,0:T(8,128)S(1)} fusion(bf16[128,24,2,384]{3,2,1,0:T(2,128)(2,1)} %bitcast.3769, pred[128,24]{1,0:T(8,128)(4,1)S(1)} %copy.12, pred[128,24]{1,0:T(8,128)(4,1)S(1)} %iota_compare_fusion.24, f32[24,24]{1,0:T(8,128)S(1)} %fusion.113), kind=kOutput, calls=%fused_computation.59 | convolution fusion | flops 118112256 | bytes 5316864 | tf_op jit(solution)/shard_map/prkw,prjw->prkj/dot_general | solution.py:73
  99.4 1.8 copy.17
  101.2 1.7 multiply_subtract_fusion.16
  102.9 1.6 fusion.1078
  104.5 1.7 fusion.1077
  106.2 1.7 fusion.1076
  107.9 1.7 fusion.1071
  109.6 4.5 %fusion.2 = f32[2,128,1,24]{3,2,1,0:T(1,128)S(1)} fusion(bf16[128,24,2,384]{3,2,1,0:T(2,128)(2,1)} %bitcast.3770, pred[128,24]{1,0:T(8,128)(4,1)S(1)} %iota_compare_fusion.24, pred[128,24]{1,0:T(8,128)(4,1)S(1)} %copy.12, bf16[2,128,384,1]{2,1,0,3:T(8,128)(2,1)} %bitcast.3809), kind=kOutput, calls=%fused_computation.3 | convolution fusion | flops 9437184 | bytes 4945920 | tf_op jit(solution)/shard_map/prkw,prw->prk/dot_general | solution.py:75
  114.9 1.2 fusion.936
  118.8 0.8 multiply_subtract_fusion.20
  119.5 0.6 multiply_subtract_fusion.19
  120.4 2.0 subtract_divide_fusion.11
  122.8 1.4 subtract_divide_fusion.275
  124.6 0.6 subtract_divide_fusion.131
  127.6 1.1 subtract_divide_fusion.22
  128.8 1.0 subtract_divide_fusion
  129.8 2.2 stack.63
  132.1 14.1 %fusion.7 = f32[2,2560,256]{2,1,0:T(8,128)} fusion(f32[2,128,256]{2,1,0:T(8,128)S(1)} %copy-done.8, f32[2,128]{1,0:T(2,128)S(1)} %get-tuple-element.1303, f32[2,128]{1,0:T(2,128)S(1)} %get-tuple-element.1304, f32[2,128]{1,0:T(2,128)S(1)} %get-tuple-element.1305, f32[2,128]{1,0:T(2,128)S(1)} %get-tuple-element.1306, f32[2,128]{1,0:T(2,128)S(1)} %get-tuple-element.1307, ...), kind=kOutput, calls=%fused_computation.7 | convolution fusion | flops 2044067840 | bytes 13393920 | tf_op jit(solution)/shard_map/per,prc->pec/dot_general | solution.py:79
  146.2 63.4 %reduce-scatter.2.cloned.1.call-done = f32[2,160,256]{2,1,0:T(8,128)} async-done(((f32[2,2560,256]{2,1,0:T(8,128)}), f32[2,160,256]{2,1,0:T(8,128)}) %reduce-scatter.2.cloned.1.call-update) | async-done | bytes 327696 | tf_op jit(solution)/shard_map/reduce_scatter | solution.py:80
  209.6 0.8 slice.1885
  210.9 0.8 slice.2605
  211.6 1.5 collective-permute-start.2
  213.2 1.0 slice.1882
  214.1 4.6 %collective-permute-done.2 = bf16[2,16,256]{2,1,0:T(8,128)(2,1)S(1)} collective-permute-done((bf16[2,16,256]{2,1,0:T(8,128)(2,1)S(1)}, bf16[2,16,256]{2,1,0:T(8,128)(2,1)S(1)}, u32[]{:S(2)}, u32[]{:S(2)}) %collective-permute-start.2) | collective-permute-done | bytes 16416 | tf_op jit(solution)/shard_map/ppermute | solution.py:15
  218.7 0.8 fusion.112
  219.5 0.7 sub.337685
  (142 shorter events, 7.3 us)
Async XLA Ops:
  6.5 11.7 %copy-start.44 = (s32[128]{0:T(128)S(1)}, s32[128]{0:T(128)}, u32[]{:S(2)}) copy-start(s32[128]{0:T(128)} %param.9) | copy-start | bytes 1540
  6.5 54.5 %all-gather.2.cloned.1.call-start = ((), (), s32[]{:S(2)}) async-start(), calls=%async_computation.1 | async-start | bytes 4177920 | tf_op jit(solution)/shard_map/all_gather | solution.py:69
  7.7 7.7 %collective-permute-start = (bf16[2,16,384]{2,0,1:T(2,128)(2,1)S(1)}, bf16[2,16,384]{2,0,1:T(2,128)(2,1)S(1)}, u32[]{:S(2)}, u32[]{:S(2)}) collective-permute-start(bf16[2,16,384]{2,0,1:T(2,128)(2,1)S(1)} %slice.1533), channel_id=1, source_target_pairs={{240,0},{0,16},{16,32},{32,48},{48,64},{64,80},{80,96},{96,112},{1... | collective-permute-start | bytes 73736 | tf_op jit(solution)/shard_map/ppermute | solution.py:15
  9.7 7.1 %collective-permute-start.1 = (bf16[2,16,384]{2,0,1:T(2,128)(2,1)S(1)}, bf16[2,16,384]{2,0,1:T(2,128)(2,1)S(1)}, u32[]{:S(2)}, u32[]{:S(2)}) collective-permute-start(bf16[2,16,384]{2,0,1:T(2,128)(2,1)S(1)} %slice.1533), channel_id=1, source_target_pairs={{16,0},{32,16},{48,32},{64,48},{80,64},{96,80},{112,96},{128,112},... | collective-permute-start | bytes 73736 | tf_op jit(solution)/shard_map/ppermute | solution.py:15
  17.9 191.7 %reduce-scatter.2.cloned.1.call-start = ((), (), s32[]{:S(2)}) async-start(), calls=%async_computation.2 | async-start | bytes 5570560 | tf_op jit(solution)/shard_map/reduce_scatter | solution.py:80
  109.6 4.8 %copy-start = (f32[256,24,24]{0,2,1:T(8,128)S(1)}, f32[256,24,24]{0,2,1:T(8,128)}, u32[]{:S(2)}) copy-start(f32[256,24,24]{0,2,1:T(8,128)} %copy.17) | copy-start | bytes 1769476
  114.2 8.5 %copy-start.23 = (f32[1,1,256]{2,1,0:T(1,128)S(1)}, f32[1,1,256]{2,1,0:T(1,128)}, u32[]{:S(2)}) copy-start(f32[1,1,256]{2,1,0:T(1,128)} %get-tuple-element.1288) | copy-start | bytes 3076
  114.2 8.5 %copy-start.24 = (f32[1,1,256]{2,1,0:T(1,128)S(1)}, f32[1,1,256]{2,1,0:T(1,128)}, u32[]{:S(2)}) copy-start(f32[1,1,256]{2,1,0:T(1,128)} %get-tuple-element.1289) | copy-start | bytes 3076
  114.2 8.5 %copy-start.25 = (f32[1,1,256]{2,1,0:T(1,128)S(1)}, f32[1,1,256]{2,1,0:T(1,128)}, u32[]{:S(2)}) copy-start(f32[1,1,256]{2,1,0:T(1,128)} %get-tuple-element.1290) | copy-start | bytes 3076
  114.2 8.5 %copy-start.26 = (f32[1,1,256]{2,1,0:T(1,128)S(1)}, f32[1,1,256]{2,1,0:T(1,128)}, u32[]{:S(2)}) copy-start(f32[1,1,256]{2,1,0:T(1,128)} %get-tuple-element.1291) | copy-start | bytes 3076
  114.2 8.5 %copy-start.27 = (f32[1,1,256]{2,1,0:T(1,128)S(1)}, f32[1,1,256]{2,1,0:T(1,128)}, u32[]{:S(2)}) copy-start(f32[1,1,256]{2,1,0:T(1,128)} %get-tuple-element.1292) | copy-start | bytes 3076
  114.2 8.5 %copy-start.28 = (f32[1,1,256]{2,1,0:T(1,128)S(1)}, f32[1,1,256]{2,1,0:T(1,128)}, u32[]{:S(2)}) copy-start(f32[1,1,256]{2,1,0:T(1,128)} %get-tuple-element.1293) | copy-start | bytes 3076
  114.3 8.5 %copy-start.29 = (f32[1,1,256]{2,1,0:T(1,128)S(1)}, f32[1,1,256]{2,1,0:T(1,128)}, u32[]{:S(2)}) copy-start(f32[1,1,256]{2,1,0:T(1,128)} %get-tuple-element.1294) | copy-start | bytes 3076
  114.3 8.5 %copy-start.30 = (f32[1,1,256]{2,1,0:T(1,128)S(1)}, f32[1,1,256]{2,1,0:T(1,128)}, u32[]{:S(2)}) copy-start(f32[1,1,256]{2,1,0:T(1,128)} %get-tuple-element.1295) | copy-start | bytes 3076
  114.3 8.5 %copy-start.31 = (f32[1,1,256]{2,1,0:T(1,128)S(1)}, f32[1,1,256]{2,1,0:T(1,128)}, u32[]{:S(2)}) copy-start(f32[1,1,256]{2,1,0:T(1,128)} %get-tuple-element.1296) | copy-start | bytes 3076
  114.3 8.5 %copy-start.32 = (f32[1,1,256]{2,1,0:T(1,128)S(1)}, f32[1,1,256]{2,1,0:T(1,128)}, u32[]{:S(2)}) copy-start(f32[1,1,256]{2,1,0:T(1,128)} %get-tuple-element.1298) | copy-start | bytes 3076
  114.3 8.5 %copy-start.33 = (f32[1,1,256]{2,1,0:T(1,128)S(1)}, f32[1,1,256]{2,1,0:T(1,128)}, u32[]{:S(2)}) copy-start(f32[1,1,256]{2,1,0:T(1,128)} %get-tuple-element.1299) | copy-start | bytes 3076
  114.3 8.5 %copy-start.34 = (f32[1,1,256]{2,1,0:T(1,128)S(1)}, f32[1,1,256]{2,1,0:T(1,128)}, u32[]{:S(2)}) copy-start(f32[1,1,256]{2,1,0:T(1,128)} %get-tuple-element.1269) | copy-start | bytes 3076
  114.3 8.5 %copy-start.35 = (f32[1,1,256]{2,1,0:T(1,128)S(1)}, f32[1,1,256]{2,1,0:T(1,128)}, u32[]{:S(2)}) copy-start(f32[1,1,256]{2,1,0:T(1,128)} %get-tuple-element.1270) | copy-start | bytes 3076
  114.3 8.5 %copy-start.36 = (f32[1,1,256]{2,1,0:T(1,128)S(1)}, f32[1,1,256]{2,1,0:T(1,128)}, u32[]{:S(2)}) copy-start(f32[1,1,256]{2,1,0:T(1,128)} %get-tuple-element.1271) | copy-start | bytes 3076
  114.3 8.5 %copy-start.37 = (f32[1,1,256]{2,1,0:T(1,128)S(1)}, f32[1,1,256]{2,1,0:T(1,128)}, u32[]{:S(2)}) copy-start(f32[1,1,256]{2,1,0:T(1,128)} %get-tuple-element.1272) | copy-start | bytes 3076
  114.3 8.5 %copy-start.38 = (f32[1,1,256]{2,1,0:T(1,128)S(1)}, f32[1,1,256]{2,1,0:T(1,128)}, u32[]{:S(2)}) copy-start(f32[1,1,256]{2,1,0:T(1,128)} %get-tuple-element.1273) | copy-start | bytes 3076
  114.4 8.5 %copy-start.39 = (f32[1,1,256]{2,1,0:T(1,128)S(1)}, f32[1,1,256]{2,1,0:T(1,128)}, u32[]{:S(2)}) copy-start(f32[1,1,256]{2,1,0:T(1,128)} %get-tuple-element.1274) | copy-start | bytes 3076
  114.5 8.3 %copy-start.40 = (f32[1,1,256]{2,1,0:T(1,128)S(1)}, f32[1,1,256]{2,1,0:T(1,128)}, u32[]{:S(2)}) copy-start(f32[1,1,256]{2,1,0:T(1,128)} %get-tuple-element.1275) | copy-start | bytes 3076
  114.8 9.6 %copy-start.9 = (f32[1,1,256]{2,1,0:T(1,128)S(1)}, f32[1,1,256]{2,1,0:T(1,128)}, u32[]{:S(2)}) copy-start(f32[1,1,256]{2,1,0:T(1,128)} %get-tuple-element.1162) | copy-start | bytes 3076
  114.8 9.6 %copy-start.10 = (f32[1,1,256]{2,1,0:T(1,128)S(1)}, f32[1,1,256]{2,1,0:T(1,128)}, u32[]{:S(2)}) copy-start(f32[1,1,256]{2,1,0:T(1,128)} %get-tuple-element.1163) | copy-start | bytes 3076
  114.8 9.6 %copy-start.11 = (f32[1,1,256]{2,1,0:T(1,128)S(1)}, f32[1,1,256]{2,1,0:T(1,128)}, u32[]{:S(2)}) copy-start(f32[1,1,256]{2,1,0:T(1,128)} %get-tuple-element.1164) | copy-start | bytes 3076
  114.8 9.6 %copy-start.12 = (f32[1,1,256]{2,1,0:T(1,128)S(1)}, f32[1,1,256]{2,1,0:T(1,128)}, u32[]{:S(2)}) copy-start(f32[1,1,256]{2,1,0:T(1,128)} %get-tuple-element.1165) | copy-start | bytes 3076
  114.8 9.6 %copy-start.13 = (f32[1,1,256]{2,1,0:T(1,128)S(1)}, f32[1,1,256]{2,1,0:T(1,128)}, u32[]{:S(2)}) copy-start(f32[1,1,256]{2,1,0:T(1,128)} %get-tuple-element.1166) | copy-start | bytes 3076
  114.8 9.6 %copy-start.14 = (f32[1,1,256]{2,1,0:T(1,128)S(1)}, f32[1,1,256]{2,1,0:T(1,128)}, u32[]{:S(2)}) copy-start(f32[1,1,256]{2,1,0:T(1,128)} %get-tuple-element.1167) | copy-start | bytes 3076
  114.8 9.6 %copy-start.15 = (f32[1,1,256]{2,1,0:T(1,128)S(1)}, f32[1,1,256]{2,1,0:T(1,128)}, u32[]{:S(2)}) copy-start(f32[1,1,256]{2,1,0:T(1,128)} %get-tuple-element.1168) | copy-start | bytes 3076
  114.8 9.6 %copy-start.16 = (f32[1,1,256]{2,1,0:T(1,128)S(1)}, f32[1,1,256]{2,1,0:T(1,128)}, u32[]{:S(2)}) copy-start(f32[1,1,256]{2,1,0:T(1,128)} %get-tuple-element.1169) | copy-start | bytes 3076
  114.8 9.6 %copy-start.17 = (f32[1,1,256]{2,1,0:T(1,128)S(1)}, f32[1,1,256]{2,1,0:T(1,128)}, u32[]{:S(2)}) copy-start(f32[1,1,256]{2,1,0:T(1,128)} %get-tuple-element.1170) | copy-start | bytes 3076
  114.9 9.6 %copy-start.18 = (f32[1,1,256]{2,1,0:T(1,128)S(1)}, f32[1,1,256]{2,1,0:T(1,128)}, u32[]{:S(2)}) copy-start(f32[1,1,256]{2,1,0:T(1,128)} %get-tuple-element.1171) | copy-start | bytes 3076
  114.9 9.6 %copy-start.19 = (f32[1,1,256]{2,1,0:T(1,128)S(1)}, f32[1,1,256]{2,1,0:T(1,128)}, u32[]{:S(2)}) copy-start(f32[1,1,256]{2,1,0:T(1,128)} %get-tuple-element.1172) | copy-start | bytes 3076
  114.9 9.6 %copy-start.20 = (f32[1,1,256]{2,1,0:T(1,128)S(1)}, f32[1,1,256]{2,1,0:T(1,128)}, u32[]{:S(2)}) copy-start(f32[1,1,256]{2,1,0:T(1,128)} %get-tuple-element.1173) | copy-start | bytes 3076
  114.9 9.6 %copy-start.21 = (f32[1,1,256]{2,1,0:T(1,128)S(1)}, f32[1,1,256]{2,1,0:T(1,128)}, u32[]{:S(2)}) copy-start(f32[1,1,256]{2,1,0:T(1,128)} %get-tuple-element.1174) | copy-start | bytes 3076
  114.9 9.6 %copy-start.22 = (f32[1,1,256]{2,1,0:T(1,128)S(1)}, f32[1,1,256]{2,1,0:T(1,128)}, u32[]{:S(2)}) copy-start(f32[1,1,256]{2,1,0:T(1,128)} %get-tuple-element.1175) | copy-start | bytes 3076
  120.4 11.6 %copy-start.1 = (pred[2560,128]{1,0:T(8,128)(4,1)S(1)}, pred[2560,128]{1,0:T(8,128)(4,1)}, u32[]{:S(2)}) copy-start(pred[2560,128]{1,0:T(8,128)(4,1)} %get-tuple-element.1380) | copy-start | bytes 983044
  120.4 11.6 %copy-start.2 = (pred[2560,128]{1,0:T(8,128)(4,1)S(1)}, pred[2560,128]{1,0:T(8,128)(4,1)}, u32[]{:S(2)}) copy-start(pred[2560,128]{1,0:T(8,128)(4,1)} %get-tuple-element.1381) | copy-start | bytes 983044
  120.4 11.6 %copy-start.3 = (pred[2560,128]{1,0:T(8,128)(4,1)S(1)}, pred[2560,128]{1,0:T(8,128)(4,1)}, u32[]{:S(2)}) copy-start(pred[2560,128]{1,0:T(8,128)(4,1)} %get-tuple-element.1382) | copy-start | bytes 983044
  120.4 11.6 %copy-start.4 = (pred[2560,128]{1,0:T(8,128)(4,1)S(1)}, pred[2560,128]{1,0:T(8,128)(4,1)}, u32[]{:S(2)}) copy-start(pred[2560,128]{1,0:T(8,128)(4,1)} %get-tuple-element.1383) | copy-start | bytes 983044
  120.4 11.6 %copy-start.5 = (pred[2560,128]{1,0:T(8,128)(4,1)S(1)}, pred[2560,128]{1,0:T(8,128)(4,1)}, u32[]{:S(2)}) copy-start(pred[2560,128]{1,0:T(8,128)(4,1)} %get-tuple-element.1384) | copy-start | bytes 983044
  120.4 11.6 %copy-start.6 = (pred[2560,128]{1,0:T(8,128)(4,1)S(1)}, pred[2560,128]{1,0:T(8,128)(4,1)}, u32[]{:S(2)}) copy-start(pred[2560,128]{1,0:T(8,128)(4,1)} %get-tuple-element.1385) | copy-start | bytes 983044
  120.4 11.6 %copy-start.7 = (pred[2560,128]{1,0:T(8,128)(4,1)S(1)}, pred[2560,128]{1,0:T(8,128)(4,1)}, u32[]{:S(2)}) copy-start(pred[2560,128]{1,0:T(8,128)(4,1)} %get-tuple-element.1386) | copy-start | bytes 983044
  120.4 11.6 %copy-start.8 = (f32[2,128,256]{2,1,0:T(8,128)S(1)}, f32[2,128,256]{2,1,0:T(8,128)}, u32[]{:S(2)}) copy-start(f32[2,128,256]{2,1,0:T(8,128)} %param.7) | copy-start | bytes 786436
  210.4 8.3 %collective-permute-start.3 = (f32[2,16,256]{2,1,0:T(8,128)S(1)}, f32[2,16,256]{2,1,0:T(8,128)S(1)}, u32[]{:S(2)}, u32[]{:S(2)}) collective-permute-start(f32[2,16,256]{2,1,0:T(8,128)S(1)} %slice.1885), channel_id=1, source_target_pairs={{240,0},{0,16},{16,32},{32,48},{48,64},{64,80},{80,96},{96,112},{1... | collective-permute-start | bytes 98312 | tf_op jit(solution)/shard_map/ppermute | solution.py:15
  211.6 7.1 %collective-permute-start.2 = (bf16[2,16,256]{2,1,0:T(8,128)(2,1)S(1)}, bf16[2,16,256]{2,1,0:T(8,128)(2,1)S(1)}, u32[]{:S(2)}, u32[]{:S(2)}) collective-permute-start(bf16[2,16,256]{2,1,0:T(8,128)(2,1)S(1)} %slice.2605), channel_id=1, source_target_pairs={{16,0},{32,16},{48,32},{64,48},{80,64},{96,80},{112,96},{128,112},... | collective-permute-start | bytes 49160 | tf_op jit(solution)/shard_map/ppermute | solution.py:15
  (3 other events, 13.6 us)
Sparse Core Ops, SparseCore 0:
  18.0 43.0 all-gather.1
  146.3 63.2 reduce-scatter.1
where the time goes:
time: 228 us; the launch traced here: 227 us
  waiting for transfers between devices  99.8 us (44%)
  local copies, waits for them, and re-layouts  47.3 us (21%)
  other arithmetic  34.7 us (15%)
  matrix products  26.6 us (12%)
  between operations  14.4 us (6%)
  starting transfers between devices  4.17 us (2%)
    reduce_scatter x1, waiting for transfers between devices, local(): mine = lax.psum_scatter(partial_sum, 'dev', scatter_dimension=1, tiled=True)  63.4 us
    all_gather x1, waiting for transfers between devices, local(): pool = lax.all_gather(extended, 'dev', axis=1, tiled=True)  30.4 us
    gather x1, local copies, waits for them, and re-layouts, local(): near = jnp.take(pool, pattern, axis=1)  30.3 us
    eq x12, other arithmetic, weight_table(): match = where_int[:, slot][None, :] == entry_ids  14.6 us
    dot_general x1, matrix products, local(): jnp.einsum('per,prc->pec', table, adj_rhs, precision=lax.Precision.HIGHEST)  14.1 us
    dot_general x1, matrix products, local(): jnp.einsum('prkw,prjw->prkj', near, near, preferred_element_type=jnp.floa...  8.01 us
    slice x15, local copies, waits for them, and re-layouts, small_solve(): acc = matrix[below, col]  6.89 us
    ppermute x4, waiting for transfers between devices, passed_along(): return lax.ppermute(block, axis, route)  5.99 us
  transfers between devices with their start and end apart: 6, of which 4 were waited for; matrix products, arithmetic and copies ran while one was open for 9% of the time, Pallas kernels for 0%

commit v1 on v0

v1 whole, which is shorter than its diff:
```python
import functools

import jax
import jax.numpy as jnp
from jax import lax
from jax.experimental import pallas as pl
from jax.experimental.pallas import tpu as pltpu
from jax.sharding import PartitionSpec as P

GHOST = 16
ridge_share = 0.25

MESH = pl.DeviceIdType.MESH
F32 = jnp.float32
BF16 = jnp.bfloat16
MEMBERS = 5
LANES = 128
PER_STEP = 832


class Copies:
    def __init__(self, send, recv):
        self.send, self.recv, self.started = send, recv, []

    def start(self, src, dst, device):
        at = len(self.started)
        copy = pltpu.make_async_remote_copy(
            src_ref=src, dst_ref=dst, send_sem=self.send.at[at], recv_sem=self.recv.at[at],
            device_id=device, device_id_type=MESH,
        )
        copy.start()
        self.started.append(copy)
        return at

    def arrived(self, at, dst, device):
        pltpu.make_async_remote_copy(
            src_ref=dst, dst_ref=dst, send_sem=self.send.at[at], recv_sem=self.recv.at[at],
            device_id=device, device_id_type=MESH,
        ).wait_recv()

    def finish(self):
        for copy in self.started:
            copy.wait_send()


def kernel(dims, rows_ref, adj_ref, pat_ref, out_ref, pool, ghost, idxb, near, adjg, adj_low, coefg, gram, mat,
           tbuf, acc, back, send_sems, recv_sems):
    n_grp, n_dev, points, own, width, slots, objs = dims
    n_z = n_dev // 2
    far = n_z // 2
    ext = own + 2 * GHOST
    n_groups = near.shape[0] // LANES
    me_g, me_d = lax.axis_index("grp"), lax.axis_index("dev")
    z, c = lax.div(me_d, 2), lax.rem(me_d, 2)
    other = 1 - c

    def chip(step):
        return lax.rem(z + step + n_z, n_z)

    right = {"dev": chip(1) * 2 + c}
    left = {"dev": chip(-1) * 2 + c}
    partner = {"dev": z * 2 + other}
    above = {"grp": lax.rem(me_g + 1, n_grp)}
    below = {"grp": lax.rem(me_g + n_grp - 1, n_grp)}
    ring = (right, left)
    copies = Copies(send_sems, recv_sems)

    barrier = pltpu.get_barrier_semaphore()
    for device in (right, left, partner, above, below):
        pl.semaphore_signal(barrier, inc=1, device_id=device, device_id_type=MESH)

    def block(zz, cc, at=0, size=None):
        size = own if size is None else size
        return pool.at[zz, pl.ds(pl.multiple_of(cc * own + at, 16), size), :]

    for p in range(points):
        pool[z, pl.ds(pl.multiple_of(c * own, own), own), p * width : (p + 1) * width] = rows_ref[p]
    pl.semaphore_wait(barrier, 5)

    half = own // 2
    waiting_ghost = []

    def pass_ghost(zz, cc):
        at = pl.ds(pl.multiple_of((zz * 2 + cc) * GHOST, GHOST), GHOST)
        src = block(zz, cc, 0, GHOST)
        waiting_ghost.append((copies.start(src, ghost.at[0, at, :], above), 0, at, above))
        waiting_ghost.append((copies.start(src, ghost.at[1, at, :], below), 1, at, below))

    def forward_row(flow, zz, part):
        ref = block(zz, c, part * half, half)
        return copies.start(ref, ref, ring[flow])

    def share_row(zz):
        ref = block(zz, c)
        return copies.start(ref, ref, partner)

    pieces = {}
    for part in (0, 1):
        for flow in (0, 1):
            if far > 1 or part == flow:
                pieces[flow, part] = forward_row(flow, z, part)
    shared = [(share_row(z), z)]
    pass_ghost(z, c)

    pat = pat_ref[...]
    owner = jnp.floor((pat + 0.5) * (1.0 / ext))
    inside = pat - owner * ext
    place = jnp.where(
        inside < own,
        owner * own + inside,
        jnp.where(inside < own + GHOST, owner * GHOST + inside + (n_dev * own - own),
                  owner * GHOST + inside + (n_dev * (own + GHOST) - own - GHOST)),
    )
    place = jnp.where(pat < 0, -1.0, place)
    first_own = (me_d * own).astype(F32)
    sub8 = lax.broadcasted_iota(jnp.int32, (8, LANES), 0).astype(F32)

    def fill_index(m, carry):
        rolled = pltpu.roll(place, lax.rem(LANES - m, LANES), 1)
        base = pl.multiple_of(m * LANES, LANES)
        for member in range(MEMBERS):
            first = member * n_groups
            column = jnp.broadcast_to(rolled[:, first : first + 1], (slots, LANES))
            if first + n_groups > own:
                column = jnp.where(first + m < own, column, -1.0)
            idxb[pl.ds(base + member * slots, slots), :] = column
        mine = sub8 * n_groups + m.astype(F32)
        mine = jnp.where((sub8 < MEMBERS) & (mine < own), mine + first_own, -1.0)
        idxb[pl.ds(base + MEMBERS * slots, 8), :] = mine
        return carry

    lax.fori_loop(0, n_groups, fill_index, 0)

    code_rows = 16
    adj_rows = own + code_rows

    def adj_block(zz, at=0, size=None):
        size = adj_rows if size is None else size
        return adjg.at[zz, pl.ds(pl.multiple_of(c * adj_rows + at, 16), size), :]

    adj_at = pl.ds(pl.multiple_of(code_rows + c * own, 16), own)
    for p in range(points):
        cut = slice(p * objs, (p + 1) * objs)
        high = adj_ref[p].astype(BF16)
        adjg[z, adj_at, cut] = high
        adj_low[:, cut] = (adj_ref[p] - high.astype(F32)).astype(BF16)
    code_at = pl.ds(pl.multiple_of(c * (2 * own + code_rows), 16), code_rows)
    for j in range(slots // 8):
        cut = slice(8 * j, 8 * j + 8)
        codes = jnp.concatenate([owner[cut], inside[cut]], axis=0)
        adjg[z, code_at, j * LANES : (j + 1) * LANES] = codes.astype(BF16)

    def add_tiles(tiles, first=False):
        def body(step, carry):
            at = pl.ds(pl.multiple_of(step * PER_STEP, PER_STEP), PER_STEP)
            index = idxb[at, :]
            total = None
            for load, base, depth in tiles:
                base = jnp.asarray(base, jnp.int32).astype(F32)
                relative = index - base
                parts = []
                for lane in range(0, depth, LANES):
                    wide = min(LANES, depth - lane)
                    lanes = (lax.broadcasted_iota(jnp.int32, (PER_STEP, wide), 1) + lane).astype(F32)
                    parts.append(jnp.where(relative[:, :wide] == lanes, 1.0, 0.0).astype(BF16))
                hot = parts[0] if len(parts) == 1 else jnp.concatenate(parts, axis=1)
                product = jnp.dot(hot, load(), preferred_element_type=F32)
                total = product if total is None else total + product
            total = total.astype(BF16)
            near[at, :] = total if first else near[at, :] + total
            return carry

        lax.fori_loop(0, near.shape[0] // PER_STEP, body, 0)

    def chip_tile(zz):
        return (lambda: pool[zz]), zz * (2 * own), 2 * own

    def take_shared(found):
        for at, zz in found:
            copies.arrived(at, block(zz, other), partner)
            pass_ghost(zz, other)

    take_shared(shared)
    add_tiles([chip_tile(z)], first=True)
    for hop in range(1, far + 1):
        last = hop == far
        from_left, from_right = chip(-hop), chip(hop)
        later = {}
        shared = []
        for part in (0, 1):
            for flow, zz in ((0, from_left), (1, from_right)):
                if (flow, part) not in pieces:
                    continue
                copies.arrived(pieces[flow, part], block(zz, c, part * half, half), ring[flow])
                if hop < far - 1 or (hop == far - 1 and part == flow):
                    later[flow, part] = forward_row(flow, zz, part)
                if not last and part == 0:
                    pass_ghost(zz, c)
        if last:
            shared.append((share_row(from_left), from_left))
            pass_ghost(from_left, c)
        else:
            shared.append((share_row(from_left), from_left))
            shared.append((share_row(from_right), from_right))
        pieces = later
        if last:
            break
        take_shared(shared)
        add_tiles([chip_tile(from_left), chip_tile(from_right)])

    adj_first = adj_rows // 2 // 16 * 16
    adj_cut = ((0, adj_first), (adj_first, adj_rows - adj_first))
    adj_state = {"sent": {}, "shared": []}

    def adj_send(zz, hop):
        for flow, block_of in zz:
            if hop == far:
                ref = adj_block(block_of, *adj_cut[flow])
            else:
                ref = adj_block(block_of)
            adj_state["sent"][flow, hop] = copies.start(ref, ref, ring[flow])

    def adj_share(zz):
        ref = adj_block(zz)
        adj_state["shared"].append((copies.start(ref, ref, partner), zz))

    def adj_step(hop):
        both = ((0, chip(-hop)), (1, chip(hop)))
        for flow, zz in both:
            ref = adj_block(zz, *adj_cut[flow]) if hop == far else adj_block(zz)
            copies.arrived(adj_state["sent"][flow, hop], ref, ring[flow])
            if hop < far:
                adj_send([(flow, zz)], hop + 1)
                adj_share(zz)
        if hop == far:
            adj_share(chip(hop))

    adj_send([(0, z), (1, z)], 1)
    adj_share(z)
    take_shared(shared)
    add_tiles([chip_tile(chip(far))])
    adj_step(1)
    for at, side, where, device in waiting_ghost:
        copies.arrived(at, ghost.at[side, where, :], device)
    side_rows = n_dev * GHOST
    add_tiles([
        ((lambda: ghost[0]), n_dev * own, side_rows),
        ((lambda: ghost[1]), n_dev * own + side_rows, side_rows),
    ])
    if far >= 2:
        adj_step(2)

    lane = lax.broadcasted_iota(jnp.int32, (slots, LANES), 1)
    sub = lax.broadcasted_iota(jnp.int32, (slots, LANES), 0)
    ridge = jnp.zeros((slots, LANES), F32)
    for member in range(MEMBERS):
        ridge = jnp.where(lane - member * slots == sub, ridge_share * width, ridge)
    lane8 = lax.broadcasted_iota(jnp.int32, (8, LANES), 1)
    row8 = lax.broadcasted_iota(jnp.int32, (8, LANES), 0)
    own_mask = (lane8 >= row8 * slots) & (lane8 < row8 * slots + slots)

    def make_gram(m, carry):
        tile = near[pl.ds(pl.multiple_of(m * LANES, LANES), LANES), :]
        for p in range(points):
            part = tile[:, p * width : (p + 1) * width]
            full = lax.dot_general(part, part, (((1,), (1,)), ((), ())), preferred_element_type=F32)
            packed = full[:slots]
            for member in range(1, MEMBERS):
                packed = jnp.where(lane >= member * slots, full[member * slots : (member + 1) * slots], packed)
            at = (p * 32 + m) * 32
            gram[pl.ds(pl.multiple_of(at, 32), slots), :] = packed + ridge
            target = jnp.sum(jnp.where(own_mask, full[MEMBERS * slots :], 0.0), axis=0, keepdims=True)
            gram[pl.ds(pl.multiple_of(at + slots, 8), 8), :] = jnp.broadcast_to(target, (8, LANES))
        return carry

    lax.fori_loop(0, n_groups, make_gram, 0)
    if far >= 3:
        adj_step(3)

    for i in range(slots + 1):
        turned = jnp.transpose(gram[pl.ds(i, 64, stride=32), :])
        mat[i, :, :, 0:64] = turned[: MEMBERS * slots].reshape(MEMBERS, slots, 64)

    for j0 in range(0, slots, 8):
        span = slots - j0
        at_slot = lax.broadcasted_iota(jnp.int32, (MEMBERS, span, LANES), 1) + j0

        def eliminate(step, carry):
            col = step + j0
            pivot_row = mat[col, :, j0:slots, :]
            inverse = 1.0 / mat[col, :, pl.ds(col, 1), :]
            beyond = at_slot > col
            factors = jnp.where(beyond, pivot_row * inverse, 0.0)
            for i in range(j0, slots):
                block_at = i // 8 * 8
                mat[i, :, block_at:slots, :] = (
                    mat[i, :, block_at:slots, :] - factors[:, i - j0 : i - j0 + 1, :] * pivot_row[:, block_at - j0 :, :]
                )
            rhs = mat[slots, :, pl.ds(col, 1), :]
            mat[slots, :, j0:slots, :] = mat[slots, :, j0:slots, :] - rhs * factors
            return carry

        lax.fori_loop(0, 8, eliminate, 0)

    at_slot = lax.broadcasted_iota(jnp.int32, (MEMBERS, slots, LANES), 1)
    solved = jnp.zeros((MEMBERS, slots, LANES), F32)
    for col in range(slots - 1, -1, -1):
        line = mat[col]
        inverse = 1.0 / line[:, col : col + 1, :]
        scaled = jnp.where(at_slot > col, line * inverse, 0.0)
        known = jnp.sum(scaled * solved, axis=1, keepdims=True)
        value = mat[slots, :, col : col + 1, :] * inverse - known
        solved = jnp.where(at_slot == col, value, solved)

    coef_rows = points * slots

    def coef_block(zz, cc, at=0, size=None):
        size = coef_rows if size is None else size
        return coefg.at[zz, pl.ds(pl.multiple_of(cc * coef_rows + at, 8), size), :]

    for p in range(points):
        coeff = jnp.zeros((slots, LANES), F32)
        for member in range(MEMBERS):
            first = member * n_groups
            rolled = pltpu.roll(solved[member], (first - 32 * p) % LANES, 1)
            coeff = jnp.where((lane >= first) & (lane < first + n_groups), rolled, coeff)
        coefg[z, pl.ds(pl.multiple_of(c * coef_rows + p * slots, 8), slots), :] = coeff

    def coef_send(flow, zz, hop):
        ref = coef_block(zz, c, flow * slots, slots) if hop == far else coef_block(zz, c)
        return copies.start(ref, ref, ring[flow])

    def coef_share(zz):
        ref = coef_block(zz, c)
        return copies.start(ref, ref, partner)

    sent = {flow: coef_send(flow, z, 1) for flow in (0, 1)}
    shared = [(coef_share(z), z)]
    for hop in range(4, far + 1):
        adj_step(hop)
    for at, zz in adj_state["shared"]:
        copies.arrived(at, adjg.at[zz, pl.ds(pl.multiple_of(other * adj_rows, 16), adj_rows), :], partner)

    me_f = me_d.astype(F32)
    entry = lax.broadcasted_iota(jnp.int32, (ext, LANES), 0).astype(F32)

    def make_table(slot_of, zz, cc):
        code_at = pl.multiple_of(cc * (2 * own + code_rows), 16)
        picked = []
        for j in range(slots // 8):
            codes = adjg[zz, pl.ds(code_at, code_rows), j * LANES : (j + 1) * LANES].astype(F32)
            picked.append(jnp.where(codes[:8] == me_f, codes[8:], -1.0))
        weights = coefg[zz, pl.ds(pl.multiple_of(cc * coef_rows, 8), coef_rows), :]
        tables = [jnp.zeros((ext, LANES), F32) for _ in range(points)]
        for k in range(slots):
            match = picked[k // 8][k % 8 : k % 8 + 1] == entry
            for p in range(points):
                row = p * slots + k
                tables[p] = tables[p] + jnp.where(match, weights[row : row + 1], 0.0)
        for p in range(points):
            tbuf[slot_of, p, :, pl.ds(pl.multiple_of(cc * LANES, LANES), LANES)] = tables[p]

    def multiply(slot_of, zz, first=False):
        for p in range(points):
            table = tbuf[slot_of, p]
            high = table.astype(BF16)
            low = (table - high.astype(F32)).astype(BF16)
            right_side = adjg[zz, code_rows : code_rows + 2 * own, p * objs : (p + 1) * objs]
            product = jnp.dot(high, right_side, preferred_element_type=F32)
            product += jnp.dot(low, right_side, preferred_element_type=F32)
            if first:
                mine = tbuf[slot_of, p, :, pl.ds(pl.multiple_of(c * LANES, LANES), LANES)].astype(BF16)
                product += jnp.dot(mine, adj_low[:, p * objs : (p + 1) * objs], preferred_element_type=F32)
            acc[p] = product if first else acc[p] + product

    make_table(0, z, c)
    at, zz = shared[0]
    copies.arrived(at, coef_block(zz, other), partner)
    make_table(0, z, other)
    multiply(0, z, first=True)
    for hop in range(1, far + 1):
        from_left, from_right = chip(-hop), chip(hop)
        shared, later = [], {}
        for flow, zz in ((0, from_left), (1, from_right)):
            ref = coef_block(zz, c, flow * slots, slots) if hop == far else coef_block(zz, c)
            copies.arrived(sent[flow], ref, ring[flow])
            if hop < far:
                later[flow] = coef_send(flow, zz, hop + 1)
                shared.append((coef_share(zz), zz))
        if hop == far:
            shared.append((coef_share(from_left), from_left))
        sent = later
        count = len(shared)

        def tile_of(i):
            return jnp.where(i == 0, from_left, from_right)

        def near_half(i, carry):
            make_table(i, tile_of(i), c)
            return carry

        def far_half(i, carry):
            make_table(i, tile_of(i), other)
            multiply(i, tile_of(i))
            return carry

        lax.fori_loop(0, count, near_half, 0)
        for at, zz in shared:
            copies.arrived(at, coef_block(zz, other), partner)
        lax.fori_loop(0, count, far_half, 0)

    low_rows, high_rows = acc.at[:, own : own + GHOST, :], acc.at[:, own + GHOST : ext, :]
    from_above = copies.start(low_rows, back.at[0], below)
    from_below = copies.start(high_rows, back.at[1], above)
    out_ref[...] = adj_ref[...] - acc[:, :own, :]
    copies.arrived(from_above, back.at[0], below)
    copies.arrived(from_below, back.at[1], above)
    out_ref[:, :GHOST, :] = out_ref[:, :GHOST, :] - (back[0] + back[1])
    copies.finish()


def local(rows, adj_rhs, pattern, lengths):
    points, own, width = rows.shape
    slots = pattern.shape[1]
    objs = adj_rhs.shape[2]
    n_grp, n_dev = lax.axis_size("grp"), lax.axis_size("dev")
    n_z = n_dev // 2
    n_groups = -(-own // MEMBERS)
    ext = own + 2 * GHOST
    used = jnp.arange(slots, dtype=jnp.int32)[:, None] < lengths[None, :]
    masked = jnp.where(used, pattern.T, -1).astype(F32)
    n_copies = 160
    vmem = pl.BlockSpec(memory_space=pltpu.VMEM)
    return pl.pallas_call(
        functools.partial(kernel, (n_grp, n_dev, points, own, width, slots, objs)),
        out_shape=jax.ShapeDtypeStruct(adj_rhs.shape, F32),
        in_specs=[vmem] * 3,
        out_specs=vmem,
        scratch_shapes=[
            pltpu.VMEM((n_z, 2 * own, points * width), BF16),
            pltpu.VMEM((2, n_dev * GHOST, points * width), BF16),
            pltpu.VMEM((n_groups * LANES, LANES), F32),
            pltpu.VMEM((n_groups * LANES, points * width), BF16),
            pltpu.VMEM((n_z, 2 * own + 32, points * objs), BF16),
            pltpu.VMEM((own, points * objs), BF16),
            pltpu.VMEM((n_z, 2 * points * slots, LANES), F32),
            pltpu.VMEM((64 * 32, LANES), F32),
            pltpu.VMEM((slots + 1, MEMBERS, slots, LANES), F32),
            pltpu.VMEM((2, points, ext, 2 * own), F32),
            pltpu.VMEM((points, ext, objs), F32),
            pltpu.VMEM((2, points, GHOST, objs), F32),
            pltpu.SemaphoreType.DMA((n_copies,)),
            pltpu.SemaphoreType.DMA((n_copies,)),
        ],
        compiler_params=pltpu.CompilerParams(
            collective_id=0, has_side_effects=True, vmem_limit_bytes=48 * 1024 * 1024
        ),
    )(rows, adj_rhs, masked)


def solution(mesh):
    placed = (
        P(None, ("grp", "dev"), None),
        P(None, ("grp", "dev"), None),
        P(("grp", "dev"), None),
        P(("grp", "dev")),
    )
    return jax.shard_map(
        local, mesh=mesh, in_specs=placed, out_specs=P(None, ("grp", "dev"), None), check_vma=False
    )
```

time: 228 us -> 77.1 us (0.34)
  the two profiles are of different devices: /device:TPU:30 before, /device:TPU:1 now
where the time goes in v1:
time: 77.1 us; the launch traced here: 77 us
  Pallas kernels  73.7 us (96%)
  local copies, waits for them, and re-layouts  2.58 us (3%)
    pallas_call x1, Pallas kernels, local(): pl.pallas_call(functools.partial(kernel, (n_grp, n_dev, points, own, widt...  73.7 us
    unnamed x5, local copies, waits for them, and re-layouts  2.58 us

profile of v1, /device:TPU:1, one launch (start us, length us, event | category | flops | bytes accessed | tf_op | source)
XLA Modules:
  0.0 77.0 jit_solution(10678736959910162772)
XLA Ops:
  0.0 0.7 fusion.pat_ref
  0.7 0.0 copy-start
  0.7 0.9 %copy-done = f32[2,128,256]{2,1,0:T(8,128)S(1)} copy-done((f32[2,128,256]{2,1,0:T(8,128)S(1)}, f32[2,128,256]{2,1,0:T(8,128)}, u32[]{:S(2)}) %copy-start) | copy-done | bytes 262168
  1.7 0.0 copy-start.1
  1.7 0.9 %copy-done.1 = bf16[2,128,384]{2,1,0:T(8,128)(2,1)S(1)} copy-done((bf16[2,128,384]{2,1,0:T(8,128)(2,1)S(1)}, bf16[2,128,384]{2,1,0:T(8,128)(2,1)}, u32[]{:S(2)}) %copy-start.1) | copy-done | bytes 196632
  2.6 73.7 %shard_map.46 = f32[2,128,256]{2,1,0:T(8,128)S(1)} custom-call(bf16[2,128,384]{2,1,0:T(8,128)(2,1)S(1)} %copy-done.1, f32[2,128,256]{2,1,0:T(8,128)S(1)} %copy-done, f32[24,128]{1,0:T(8,128)S(1)} %fusion.pat_ref), custom_call_target="tpu_custom_call" | custom-call | tf_op jit(solution)/shard_map/pallas_call | solution.py:434
  76.3 0.7 copy.6
Async XLA Ops:
  0.7 1.0 %copy-start = (f32[2,128,256]{2,1,0:T(8,128)S(1)}, f32[2,128,256]{2,1,0:T(8,128)}, u32[]{:S(2)}) copy-start(f32[2,128,256]{2,1,0:T(8,128)} %adj_ref.1) | copy-start | bytes 786436
  1.7 0.9 %copy-start.1 = (bf16[2,128,384]{2,1,0:T(8,128)(2,1)S(1)}, bf16[2,128,384]{2,1,0:T(8,128)(2,1)}, u32[]{:S(2)}) copy-start(bf16[2,128,384]{2,1,0:T(8,128)(2,1)} %rows_ref.1) | copy-start | bytes 589828

commit v2 on v1

v2 whole, which is shorter than its diff:
```python
import functools

import jax
import jax.numpy as jnp
from jax import lax
from jax.experimental import pallas as pl
from jax.experimental.pallas import tpu as pltpu
from jax.sharding import PartitionSpec as P

GHOST = 16
ridge_share = 0.25

MESH = pl.DeviceIdType.MESH
F32 = jnp.float32
BF16 = jnp.bfloat16
MEMBERS = 5
LANES = 128
PER_STEP = 3328
UNROLL_INDEX = 13
TURNS = 4
UNROLL_GRAM = 13


class Copies:
    def __init__(self, send, recv):
        self.send, self.recv, self.started, self.gone = send, recv, [], set()

    def start(self, src, dst, device):
        at = len(self.started)
        copy = pltpu.make_async_remote_copy(
            src_ref=src, dst_ref=dst, send_sem=self.send.at[at], recv_sem=self.recv.at[at],
            device_id=device, device_id_type=MESH,
        )
        copy.start()
        self.started.append(copy)
        return at

    def arrived(self, at, dst, device):
        pltpu.make_async_remote_copy(
            src_ref=dst, dst_ref=dst, send_sem=self.send.at[at], recv_sem=self.recv.at[at],
            device_id=device, device_id_type=MESH,
        ).wait_recv()

    def left(self, at):
        self.started[at].wait_send()
        self.gone.add(at)

    def finish(self):
        for at, copy in enumerate(self.started):
            if at not in self.gone:
                copy.wait_send()


def kernel(dims, rows_ref, adj_ref, pat_ref, len_ref, out_ref, pool, ghost, idxb, near, adjg, adj_low, coefg, gram, mat,
           tall, adj_own, acc, back, send_sems, recv_sems, load_sems):
    n_grp, n_dev, points, own, width, slots, objs = dims
    n_z = n_dev // 2
    far = n_z // 2
    ext = own + 2 * GHOST
    n_groups = near.shape[0] // LANES
    me_g, me_d = lax.axis_index("grp"), lax.axis_index("dev")
    z, c = lax.div(me_d, 2), lax.rem(me_d, 2)
    other = 1 - c

    def chip(step):
        return lax.rem(z + step + n_z, n_z)

    def peer(step):
        return {"dev": chip(step) * 2 + c}

    right, left = peer(1), peer(-1)
    partner = {"dev": z * 2 + other}
    above, below = lax.rem(me_g + 1, n_grp), lax.rem(me_g + n_grp - 1, n_grp)
    sides = (above, below)
    ring = (right, left)
    copies = Copies(send_sems, recv_sems)

    barrier = pltpu.get_barrier_semaphore()
    greeted = [peer(step) for step in range(1, n_z)] + [partner]
    for side in sides:
        greeted += [{"grp": side}, {"grp": side, "dev": z * 2 + other}, {"grp": side, "dev": chip(far) * 2 + c}]
    for device in greeted:
        pl.semaphore_signal(barrier, inc=1, device_id=device, device_id_type=MESH)

    def block(zz, cc, at=0, size=None):
        size = own if size is None else size
        return pool.at[zz, pl.ds(pl.multiple_of(cc * own + at, 16), size), :]

    mine_at = pl.ds(pl.multiple_of(c * own, own), own)
    loads = [
        pltpu.make_async_copy(rows_ref.at[p], pool.at[z, mine_at, pl.ds(p * width, width)], load_sems.at[p])
        for p in range(points)
    ]
    adj_load = pltpu.make_async_copy(adj_ref, adj_own, load_sems.at[points])
    for load in loads:
        load.start()
    adj_load.start()
    pat = pat_ref[...].astype(F32)
    pat = jnp.transpose(jnp.concatenate([pat, jnp.zeros((own, LANES - slots), F32)], axis=1))[:slots]
    slot_of = lax.broadcasted_iota(jnp.int32, (slots, own), 0)
    pat = jnp.where(slot_of < len_ref[...], pat, -1.0)
    owner = jnp.floor((pat + 0.5) * (1.0 / ext))
    inside = pat - owner * ext
    place = jnp.where(
        inside < own,
        owner * own + inside,
        jnp.where(inside < own + GHOST, owner * GHOST + inside + (n_dev * own - own),
                  owner * GHOST + inside + (n_dev * (own + GHOST) - own - GHOST)),
    )
    place = jnp.where(pat < 0, -1.0, place)
    first_own = (me_d * own).astype(F32)
    sub8 = lax.broadcasted_iota(jnp.int32, (8, LANES), 0).astype(F32)

    def fill_index(m, carry):
        rolled = pltpu.roll(place, lax.rem(LANES - m, LANES), 1)
        base = pl.multiple_of(m * LANES, LANES)
        for member in range(MEMBERS):
            first = member * n_groups
            column = jnp.broadcast_to(rolled[:, first : first + 1], (slots, LANES))
            if first + n_groups > own:
                column = jnp.where(first + m < own, column, -1.0)
            idxb[pl.ds(base + member * slots, slots), :] = column
        mine = sub8 * n_groups + jnp.asarray(m, jnp.int32).astype(F32)
        mine = jnp.where((sub8 < MEMBERS) & (mine < own), mine + first_own, -1.0)
        idxb[pl.ds(base + MEMBERS * slots, 8), :] = mine
        return carry

    lax.fori_loop(0, n_groups, fill_index, 0, unroll=UNROLL_INDEX)

    code_rows = 16
    adj_rows = own + code_rows

    def adj_block(zz, cc, at=0, size=None):
        size = adj_rows if size is None else size
        return adjg.at[zz, pl.ds(pl.multiple_of(cc * adj_rows + at, 16), size), :]

    adj_load.wait()
    adj_at = pl.ds(pl.multiple_of(code_rows + c * own, 16), own)
    for p in range(points):
        cut = slice(p * objs, (p + 1) * objs)
        high = adj_own[p].astype(BF16)
        adjg[z, adj_at, cut] = high
        adj_low[:, cut] = (adj_own[p] - high.astype(F32)).astype(BF16)
    code_at = pl.ds(pl.multiple_of(c * (2 * own + code_rows), 16), code_rows)
    for j in range(slots // 8):
        cut = slice(8 * j, 8 * j + 8)
        codes = jnp.concatenate([owner[cut], inside[cut]], axis=0)
        adjg[z, code_at, j * LANES : (j + 1) * LANES] = codes.astype(BF16)

    for load in loads:
        load.wait()
    pl.semaphore_wait(barrier, len(greeted))

    piece = own // TURNS
    waiting_ghost = []

    def ghost_at(zz, cc):
        return pl.ds(pl.multiple_of((zz * 2 + cc) * GHOST, GHOST), GHOST)

    def pass_ghost(zz):
        src = block(zz, c, 0, GHOST)
        for to in (0, 1):
            for cc in (c, other):
                device = {"grp": sides[to], "dev": z * 2 + cc}
                at = copies.start(src, ghost.at[to, ghost_at(zz, c), :], device)
                waiting_ghost.append((at, to, zz, cc, device))

    def forward_row(flow, zz, part):
        ref = block(zz, c, part * piece, piece)
        return copies.start(ref, ref, ring[flow])

    def share_row(zz):
        ref = block(zz, c)
        return copies.start(ref, ref, partner), zz

    def part_of(flow, turn):
        return TURNS - 1 - turn if flow else turn

    pieces = {}
    for turn in range(TURNS if far > 1 else TURNS // 2):
        for flow in (0, 1):
            pieces[flow, turn] = forward_row(flow, z, part_of(flow, turn))
    shared = [share_row(z)]
    far_ghost = []
    for to in (0, 1):
        device = {"grp": sides[to], "dev": chip(far) * 2 + c}
        far_ghost.append((copies.start(block(z, c, 0, GHOST), ghost.at[to, ghost_at(z, c), :], device), to, device))
    pass_ghost(z)
    def add_tile(load, base, depth, first=False):
        base = jnp.asarray(base, jnp.int32).astype(F32)

        def body(step, carry):
            at = pl.ds(pl.multiple_of(step * PER_STEP, PER_STEP), PER_STEP)
            relative = idxb[at, :] - base
            parts = []
            for lane in range(0, depth, LANES):
                wide = min(LANES, depth - lane)
                lanes = (lax.broadcasted_iota(jnp.int32, (PER_STEP, wide), 1) + lane).astype(F32)
                parts.append(jnp.where(relative[:, :wide] == lanes, 1.0, 0.0).astype(BF16))
            hot = parts[0] if len(parts) == 1 else jnp.concatenate(parts, axis=1)
            total = jnp.dot(hot, load(), preferred_element_type=F32).astype(BF16)
            near[at, :] = total if first else near[at, :] + total
            return carry

        lax.fori_loop(0, near.shape[0] // PER_STEP, body, 0)

    def chip_tile(zz, first=False):
        add_tile(lambda: pool[zz], zz * (2 * own), 2 * own, first)

    def take_shared(found):
        for at, zz in found:
            copies.arrived(at, block(zz, other), partner)

    def take(hop, turn):
        for flow, zz in ((0, chip(-hop)), (1, chip(hop))):
            if (flow, turn) not in pieces:
                continue
            part = part_of(flow, turn)
            copies.arrived(pieces[flow, turn], block(zz, c, part * piece, piece), ring[flow])
            if hop < far - 1 or (hop == far - 1 and turn < TURNS // 2):
                later[flow, turn] = forward_row(flow, zz, part)
            if hop < far and part == 0:
                pass_ghost(zz)

    adj_first = adj_rows // 2 // 16 * 16
    adj_cut = ((0, adj_first), (adj_first, adj_rows - adj_first))
    adj_sent, adj_shared = {}, []

    def adj_send(flow, zz, hop, turn):
        ref = adj_block(zz, c, *adj_cut[turn ^ flow])
        adj_sent[flow, hop, turn] = copies.start(ref, ref, ring[flow])

    def adj_start(turn):
        if far > 1 or turn == 0:
            for flow in (0, 1):
                adj_send(flow, z, 1, turn)

    def adj_share(zz):
        ref = adj_block(zz, c)
        adj_shared.append((copies.start(ref, ref, partner), zz))

    def adj_take(hop, turn):
        if hop > far:
            return
        for flow, zz in ((0, chip(-hop)), (1, chip(hop))):
            if (flow, hop, turn) in adj_sent:
                copies.arrived(adj_sent[flow, hop, turn], adj_block(zz, c, *adj_cut[turn ^ flow]), ring[flow])
                if hop < far - 1 or (hop == far - 1 and turn == 0):
                    adj_send(flow, zz, hop + 1, turn)
            if hop < far and turn == 1:
                adj_share(zz)
        if hop == far and turn == 0:
            adj_share(chip(hop))

    if far == 1:
        adj_start(0)
    waiting_tiles = [z]
    for hop in range(1, far + 1):
        later = {}
        for turn in range(TURNS // 2):
            take(hop, turn)
        take_shared(shared)
        if hop == far:
            adj_start(1)
            adj_take(1, 0)
            shared = [share_row(chip(hop))]
            break
        chip_tile(waiting_tiles.pop(0), first=hop == 1)
        for turn in range(TURNS // 2, TURNS):
            take(hop, turn)
        pieces = later
        now = [chip(-hop), chip(hop)]
        shared = [share_row(zz) for zz in now]
        if hop == far - 1:
            adj_start(0)
        for zz in waiting_tiles:
            chip_tile(zz)
        waiting_tiles = now

    relayed = []
    for at, to, device in far_ghost:
        ref = ghost.at[to, ghost_at(chip(far), c), :]
        copies.arrived(at, ref, device)
        relayed.append((copies.start(ref, ref, partner), to))
    adj_share(z)
    chip_tile(waiting_tiles[0], first=far == 1)
    adj_take(1, 1)
    for zz in waiting_tiles[1:]:
        chip_tile(zz)
    take_shared(shared)
    chip_tile(chip(far))
    adj_take(2, 0)
    for at, to, zz, cc, device in waiting_ghost:
        copies.arrived(at, ghost.at[to, ghost_at(zz, cc), :], device)
    for at, to in relayed:
        copies.arrived(at, ghost.at[to, ghost_at(chip(far), other), :], partner)
    side_rows = n_dev * GHOST
    add_tile((lambda: ghost[0]), n_dev * own, side_rows)
    adj_take(2, 1)
    add_tile((lambda: ghost[1]), n_dev * own + side_rows, side_rows)

    lane = lax.broadcasted_iota(jnp.int32, (slots, LANES), 1)
    sub = lax.broadcasted_iota(jnp.int32, (slots, LANES), 0)
    ridge = jnp.zeros((slots, LANES), F32)
    for member in range(MEMBERS):
        ridge = jnp.where(lane - member * slots == sub, ridge_share * width, ridge)
    lane8 = lax.broadcasted_iota(jnp.int32, (8, LANES), 1)
    row8 = lax.broadcasted_iota(jnp.int32, (8, LANES), 0)
    own_mask = (lane8 >= row8 * slots) & (lane8 < row8 * slots + slots)

    def make_gram(m, carry):
        tile = near[pl.ds(pl.multiple_of(m * LANES, LANES), LANES), :]
        for p in range(points):
            part = tile[:, p * width : (p + 1) * width]
            full = lax.dot_general(part, part, (((1,), (1,)), ((), ())), preferred_element_type=F32)
            packed = full[:slots]
            for member in range(1, MEMBERS):
                packed = jnp.where(lane >= member * slots, full[member * slots : (member + 1) * slots], packed)
            at = (p * 32 + m) * 32
            gram[pl.ds(pl.multiple_of(at, 32), slots), :] = packed + ridge
            target = jnp.sum(jnp.where(own_mask, full[MEMBERS * slots :], 0.0), axis=0, keepdims=True)
            gram[pl.ds(pl.multiple_of(at + slots, 8), 8), :] = jnp.broadcast_to(target, (8, LANES))
        return carry

    lax.fori_loop(0, n_groups // 2, make_gram, 0, unroll=UNROLL_GRAM)
    adj_take(3, 0)
    lax.fori_loop(n_groups // 2, n_groups, make_gram, 0, unroll=UNROLL_GRAM)
    adj_take(3, 1)

    for i in range(slots + 1):
        turned = jnp.transpose(gram[pl.ds(i, 64, stride=32), :])
        mat[i, :, :, 0:64] = turned[: MEMBERS * slots].reshape(MEMBERS, slots, 64)

    for j0 in range(0, slots, 8):
        span = slots - j0
        at_slot = lax.broadcasted_iota(jnp.int32, (MEMBERS, span, LANES), 1) + j0

        def eliminate(step, carry):
            col = step + j0
            pivot_row = mat[col, :, j0:slots, :]
            inverse = 1.0 / mat[col, :, pl.ds(col, 1), :]
            beyond = at_slot > col
            factors = jnp.where(beyond, pivot_row * inverse, 0.0)
            for i in range(j0, slots):
                block_at = i // 8 * 8
                mat[i, :, block_at:slots, :] = (
                    mat[i, :, block_at:slots, :] - factors[:, i - j0 : i - j0 + 1, :] * pivot_row[:, block_at - j0 :, :]
                )
            rhs = mat[slots, :, pl.ds(col, 1), :]
            mat[slots, :, j0:slots, :] = mat[slots, :, j0:slots, :] - rhs * factors
            return carry

        lax.fori_loop(0, 8, eliminate, 0)
    adj_take(4, 0)
    at_slot = lax.broadcasted_iota(jnp.int32, (MEMBERS, slots, LANES), 1)
    solved = jnp.zeros((MEMBERS, slots, LANES), F32)
    for col in range(slots - 1, -1, -1):
        line = mat[col]
        inverse = 1.0 / line[:, col : col + 1, :]
        scaled = jnp.where(at_slot > col, line * inverse, 0.0)
        known = jnp.sum(scaled * solved, axis=1, keepdims=True)
        value = mat[slots, :, col : col + 1, :] * inverse - known
        solved = jnp.where(at_slot == col, value, solved)

    coef_rows = points * slots

    def coef_block(zz, cc):
        return coefg.at[zz, pl.ds(pl.multiple_of(cc * coef_rows, 8), coef_rows), :]

    for p in range(points):
        coeff = jnp.zeros((slots, LANES), F32)
        for member in range(MEMBERS):
            first = member * n_groups
            rolled = pltpu.roll(solved[member], (first - 32 * p) % LANES, 1)
            coeff = jnp.where((lane >= first) & (lane < first + n_groups), rolled, coeff)
        coefg[z, pl.ds(pl.multiple_of(c * coef_rows + p * slots, 8), slots), :] = coeff

    coef_sent = {}
    for hop in range(far, 0, -1):
        for step in (hop, -hop) if hop < far else (hop,):
            ref = coef_block(z, c)
            coef_sent[step] = copies.start(ref, ref, peer(step))

    def coef_share(zz):
        ref = coef_block(zz, c)
        return copies.start(ref, ref, partner), zz

    shared = [coef_share(z)]
    me_f = me_d.astype(F32)
    entry = lax.broadcasted_iota(jnp.int32, (ext, LANES), 0).astype(F32)

    def make_table(zz, cc):
        code_at = pl.multiple_of(cc * (2 * own + code_rows), 16)
        picked = []
        for j in range(slots // 8):
            codes = adjg[zz, pl.ds(code_at, code_rows), j * LANES : (j + 1) * LANES].astype(F32)
            picked.append(jnp.where(codes[:8] == me_f, codes[8:], -1.0))
        weights = coefg[zz, pl.ds(pl.multiple_of(cc * coef_rows, 8), coef_rows), :]
        tables = [jnp.zeros((ext, LANES), F32) for _ in range(points)]
        for k in range(slots):
            match = picked[k // 8][k % 8 : k % 8 + 1] == entry
            for p in range(points):
                row = p * slots + k
                tables[p] = tables[p] + jnp.where(match, weights[row : row + 1], 0.0)
        at = pl.ds(pl.multiple_of((zz * 2 + cc) * LANES, LANES), LANES)
        for p in range(points):
            high = tables[p].astype(BF16)
            tall[p, 0:ext, at] = high
            tall[p, ext : 2 * ext, at] = (tables[p] - high.astype(F32)).astype(BF16)

    def table_loop(hop, cc, count):
        def body(i, carry):
            make_table(jnp.where(i == 0, chip(-hop), chip(hop)), cc)
            return carry

        lax.fori_loop(0, count, body, 0)

    def take_coef(found):
        for at, zz in found:
            copies.arrived(at, coef_block(zz, other), partner)

    make_table(z, c)
    take_coef(shared)
    adj_take(4, 1)
    for hop in range(5, far + 1):
        adj_take(hop, 0)
        adj_take(hop, 1)
    for at, zz in adj_shared:
        copies.arrived(at, adj_block(zz, other), partner)
    make_table(z, other)
    own_lanes = pl.ds(pl.multiple_of(me_d * LANES, LANES), LANES)

    def multiply(zz, first=False):
        lanes = pl.ds(pl.multiple_of(zz * 2 * LANES, 2 * LANES), 2 * LANES)
        for p in range(points):
            cut = slice(p * objs, (p + 1) * objs)
            product = jnp.dot(tall[p, :, lanes], adjg[zz, code_rows : code_rows + 2 * own, cut],
                              preferred_element_type=F32)
            product = product[:ext] + product[ext:]
            if first:
                acc[p] = product + jnp.dot(tall[p, :ext, own_lanes], adj_low[:, cut], preferred_element_type=F32)
            else:
                acc[p] = acc[p] + product

    multiply(z, first=True)
    for hop in range(1, far + 1):
        shared = []
        for step in (-hop, hop) if hop < far else (hop,):
            copies.arrived(coef_sent[-step if hop < far else step], coef_block(chip(step), c), peer(step))
            shared.append(coef_share(chip(step)))
        table_loop(hop, c, len(shared))
        take_coef(shared)
        table_loop(hop, other, len(shared))
        for _, zz in shared:
            multiply(zz)

    low_rows, high_rows = acc.at[:, own : own + GHOST, :], acc.at[:, own + GHOST : ext, :]
    from_above = copies.start(low_rows, back.at[0], {"grp": below})
    from_below = copies.start(high_rows, back.at[1], {"grp": above})
    out_ref[...] = adj_own[...] - acc[:, :own, :]
    copies.arrived(from_above, back.at[0], {"grp": below})
    copies.arrived(from_below, back.at[1], {"grp": above})
    out_ref[:, :GHOST, :] = out_ref[:, :GHOST, :] - (back[0] + back[1])
    copies.finish()


def local(rows, adj_rhs, pattern, lengths):
    points, own, width = rows.shape
    slots = pattern.shape[1]
    objs = adj_rhs.shape[2]
    n_grp, n_dev = lax.axis_size("grp"), lax.axis_size("dev")
    n_z = n_dev // 2
    n_groups = -(-own // MEMBERS)
    ext = own + 2 * GHOST
    n_copies = 120
    vmem = pl.BlockSpec(memory_space=pltpu.VMEM)
    anywhere = pl.BlockSpec(memory_space=pl.ANY)
    return pl.pallas_call(
        functools.partial(kernel, (n_grp, n_dev, points, own, width, slots, objs)),
        out_shape=jax.ShapeDtypeStruct(adj_rhs.shape, F32),
        in_specs=[anywhere, anywhere, vmem, vmem],
        out_specs=vmem,
        scratch_shapes=[
            pltpu.VMEM((n_z, 2 * own, points * width), BF16),
            pltpu.VMEM((2, n_dev * GHOST, points * width), BF16),
            pltpu.VMEM((n_groups * LANES, LANES), F32),
            pltpu.VMEM((n_groups * LANES, points * width), BF16),
            pltpu.VMEM((n_z, 2 * own + 32, points * objs), BF16),
            pltpu.VMEM((own, points * objs), BF16),
            pltpu.VMEM((n_z, 2 * points * slots, LANES), F32),
            pltpu.VMEM((64 * 32, LANES), F32),
            pltpu.VMEM((slots + 1, MEMBERS, slots, LANES), F32),
            pltpu.VMEM((points, 2 * ext, n_dev * LANES), BF16),
            pltpu.VMEM((points, own, objs), F32),
            pltpu.VMEM((points, ext, objs), F32),
            pltpu.VMEM((2, points, GHOST, objs), F32),
            pltpu.SemaphoreType.DMA((n_copies,)),
            pltpu.SemaphoreType.DMA((n_copies,)),
            pltpu.SemaphoreType.DMA((points + 1,)),
        ],
        compiler_params=pltpu.CompilerParams(
            collective_id=0, has_side_effects=True, vmem_limit_bytes=48 * 1024 * 1024
        ),
    )(rows, adj_rhs, pattern, lengths.reshape(1, own))


def solution(mesh):
    placed = (
        P(None, ("grp", "dev"), None),
        P(None, ("grp", "dev"), None),
        P(("grp", "dev"), None),
        P(("grp", "dev")),
    )
    return jax.shard_map(
        local, mesh=mesh, in_specs=placed, out_specs=P(None, ("grp", "dev"), None), check_vma=False
    )
```

time: 77.1 us -> 72.2 us (0.936)
  Pallas kernels: 73.7 us -> 68.6 us
  local copies, waits for them, and re-layouts: 2.58 us -> 3.4 us
    pallas_call x1, Pallas kernels: 73.7 us -> 68.6 us  [local(): pl.pallas_call(functools.partial(kernel, (n_grp, n_dev, points, own, widt...]
    unnamed x5 -> x8, local copies, waits for them, and re-layouts: 2.58 us -> 3.4 us
where the time goes in v2:
time: 72.2 us; the launch traced here: 72.1 us
  Pallas kernels  68.6 us (95%)
  local copies, waits for them, and re-layouts  3.4 us (5%)
    pallas_call x1, Pallas kernels, local(): pl.pallas_call(functools.partial(kernel, (n_grp, n_dev, points, own, widt...  68.6 us
    unnamed x8, local copies, waits for them, and re-layouts  3.4 us

profile of v2, /device:TPU:1, one launch (start us, length us, event | category | flops | bytes accessed | tf_op | source)
XLA Modules:
  0.0 72.1 jit_solution(299810593337514101)
XLA Ops:
  0.0 0.0 copy-start.2
  0.0 0.8 %copy.5.pat_ref = s32[128,24]{1,0:T(8,128)S(1)} copy(s32[128,24]{0,1:T(8,128)} %param.6) | data formatting | bytes 24576 | tf_op args[2]
  0.8 0.0 copy-done.2
  0.8 0.0 copy-start
  0.8 0.9 %copy-done = f32[2,128,256]{2,1,0:T(8,128)S(1)} copy-done((f32[2,128,256]{2,1,0:T(8,128)S(1)}, f32[2,128,256]{2,1,0:T(8,128)}, u32[]{:S(2)}) %copy-start) | copy-done | bytes 262168
  1.8 0.0 copy-start.1
  1.8 0.9 %copy-done.1 = bf16[2,128,384]{2,1,0:T(8,128)(2,1)S(1)} copy-done((bf16[2,128,384]{2,1,0:T(8,128)(2,1)S(1)}, bf16[2,128,384]{2,1,0:T(8,128)(2,1)}, u32[]{:S(2)}) %copy-start.1) | copy-done | bytes 196632
  2.7 68.6 %shard_map.46 = f32[2,128,256]{2,1,0:T(8,128)S(1)} custom-call(bf16[2,128,384]{2,1,0:T(8,128)(2,1)S(1)} %copy-done.1, f32[2,128,256]{2,1,0:T(8,128)S(1)} %copy-done, s32[128,24]{1,0:T(8,128)S(1)} %copy.5.pat_ref, s32[1,128]{1,0:T(1,128)S(1)} %bitcast.1), custom_call_target="tpu_custom_call" | custom-call | tf_op jit(solution)/shard_map/pallas_call | solution.py:478
  71.3 0.7 copy.7
Async XLA Ops:
  0.0 0.8 %copy-start.2 = (s32[128]{0:T(128)S(1)}, s32[128]{0:T(128)}, u32[]{:S(2)}) copy-start(s32[128]{0:T(128)} %param.7) | copy-start | bytes 1540
  0.8 1.0 %copy-start = (f32[2,128,256]{2,1,0:T(8,128)S(1)}, f32[2,128,256]{2,1,0:T(8,128)}, u32[]{:S(2)}) copy-start(f32[2,128,256]{2,1,0:T(8,128)} %adj_ref.1) | copy-start | bytes 786436
  1.8 0.9 %copy-start.1 = (bf16[2,128,384]{2,1,0:T(8,128)(2,1)S(1)}, bf16[2,128,384]{2,1,0:T(8,128)(2,1)}, u32[]{:S(2)}) copy-start(bf16[2,128,384]{2,1,0:T(8,128)(2,1)} %rows_ref.1) | copy-start | bytes 589828

commit v3 on v2

--- a/solution.py
+++ b/solution.py
@@ -174,12 +174,16 @@
         return copies.start(ref, ref, partner), zz
 
     def part_of(flow, turn):
-        return TURNS - 1 - turn if flow else turn
+        return (TURNS - turn) % TURNS if flow else turn
+
+    def goes_far(flow, part):
+        return (part >= TURNS // 2) == (flow == 1)
 
     pieces = {}
-    for turn in range(TURNS if far > 1 else TURNS // 2):
+    for turn in range(TURNS):
         for flow in (0, 1):
-            pieces[flow, turn] = forward_row(flow, z, part_of(flow, turn))
+            if far > 1 or goes_far(flow, part_of(flow, turn)):
+                pieces[flow, turn] = forward_row(flow, z, part_of(flow, turn))
     shared = [share_row(z)]
     far_ghost = []
     for to in (0, 1):
@@ -217,14 +221,14 @@
                 continue
             part = part_of(flow, turn)
             copies.arrived(pieces[flow, turn], block(zz, c, part * piece, piece), ring[flow])
-            if hop < far - 1 or (hop == far - 1 and turn < TURNS // 2):
+            if hop < far - 1 or (hop == far - 1 and goes_far(flow, part)):
                 later[flow, turn] = forward_row(flow, zz, part)
             if hop < far and part == 0:
                 pass_ghost(zz)
 
     adj_first = adj_rows // 2 // 16 * 16
     adj_cut = ((0, adj_first), (adj_first, adj_rows - adj_first))
-    adj_sent, adj_shared = {}, []
+    adj_sent, adj_shared = {}, {hop: [] for hop in range(far + 1)}
 
     def adj_send(flow, zz, hop, turn):
         ref = adj_block(zz, c, *adj_cut[turn ^ flow])
@@ -235,9 +239,9 @@
             for flow in (0, 1):
                 adj_send(flow, z, 1, turn)
 
-    def adj_share(zz):
+    def adj_share(hop, zz):
         ref = adj_block(zz, c)
-        adj_shared.append((copies.start(ref, ref, partner), zz))
+        adj_shared[hop].append((copies.start(ref, ref, partner), zz))
 
     def adj_take(hop, turn):
         if hop > far:
@@ -248,47 +252,48 @@
                 if hop < far - 1 or (hop == far - 1 and turn == 0):
                     adj_send(flow, zz, hop + 1, turn)
             if hop < far and turn == 1:
-                adj_share(zz)
+                adj_share(hop, zz)
         if hop == far and turn == 0:
-            adj_share(chip(hop))
-
-    if far == 1:
+            adj_share(hop, chip(hop))
+
+    if far <= 2:
         adj_start(0)
     waiting_tiles = [z]
-    for hop in range(1, far + 1):
+    for hop in range(1, far):
         later = {}
         for turn in range(TURNS // 2):
             take(hop, turn)
         take_shared(shared)
-        if hop == far:
-            adj_start(1)
-            adj_take(1, 0)
-            shared = [share_row(chip(hop))]
-            break
         chip_tile(waiting_tiles.pop(0), first=hop == 1)
         for turn in range(TURNS // 2, TURNS):
             take(hop, turn)
         pieces = later
         now = [chip(-hop), chip(hop)]
         shared = [share_row(zz) for zz in now]
+        if hop == far - 2:
+            adj_start(0)
         if hop == far - 1:
-            adj_start(0)
+            adj_take(1, 0)
+            adj_start(1)
         for zz in waiting_tiles:
             chip_tile(zz)
         waiting_tiles = now
-
     relayed = []
     for at, to, device in far_ghost:
         ref = ghost.at[to, ghost_at(chip(far), c), :]
         copies.arrived(at, ref, device)
         relayed.append((copies.start(ref, ref, partner), to))
-    adj_share(z)
+    adj_share(0, z)
+    take_shared(shared)
     chip_tile(waiting_tiles[0], first=far == 1)
-    adj_take(1, 1)
     for zz in waiting_tiles[1:]:
         chip_tile(zz)
-    take_shared(shared)
-    chip_tile(chip(far))
+    for turn in range(TURNS):
+        take(far, turn)
+    shared = [share_row(chip(far))]
+    if far == 1:
+        adj_take(1, 0)
+    adj_take(1, 1)
     adj_take(2, 0)
     for at, to, zz, cc, device in waiting_ghost:
         copies.arrived(at, ghost.at[to, ghost_at(zz, cc), :], device)
@@ -296,8 +301,11 @@
         copies.arrived(at, ghost.at[to, ghost_at(chip(far), other), :], partner)
     side_rows = n_dev * GHOST
     add_tile((lambda: ghost[0]), n_dev * own, side_rows)
+    take_shared(shared)
+    chip_tile(chip(far))
     adj_take(2, 1)
     add_tile((lambda: ghost[1]), n_dev * own + side_rows, side_rows)
+    adj_take(3, 0)
 
     lane = lax.broadcasted_iota(jnp.int32, (slots, LANES), 1)
     sub = lax.broadcasted_iota(jnp.int32, (slots, LANES), 0)
@@ -323,7 +331,6 @@
         return carry
 
     lax.fori_loop(0, n_groups // 2, make_gram, 0, unroll=UNROLL_GRAM)
-    adj_take(3, 0)
     lax.fori_loop(n_groups // 2, n_groups, make_gram, 0, unroll=UNROLL_GRAM)
     adj_take(3, 1)
 
@@ -351,7 +358,6 @@
             return carry
 
         lax.fori_loop(0, 8, eliminate, 0)
-    adj_take(4, 0)
     at_slot = lax.broadcasted_iota(jnp.int32, (MEMBERS, slots, LANES), 1)
     solved = jnp.zeros((MEMBERS, slots, LANES), F32)
     for col in range(slots - 1, -1, -1):
@@ -376,7 +382,7 @@
         coefg[z, pl.ds(pl.multiple_of(c * coef_rows + p * slots, 8), slots), :] = coeff
 
     coef_sent = {}
-    for hop in range(far, 0, -1):
+    for hop in sorted(range(1, far + 1), key=lambda hop: hop):
         for step in (hop, -hop) if hop < far else (hop,):
             ref = coef_block(z, c)
             coef_sent[step] = copies.start(ref, ref, peer(step))
@@ -421,12 +427,12 @@
 
     make_table(z, c)
     take_coef(shared)
-    adj_take(4, 1)
-    for hop in range(5, far + 1):
-        adj_take(hop, 0)
-        adj_take(hop, 1)
-    for at, zz in adj_shared:
-        copies.arrived(at, adj_block(zz, other), partner)
+
+    def take_adj(hop):
+        for at, zz in adj_shared[hop]:
+            copies.arrived(at, adj_block(zz, other), partner)
+
+    take_adj(0)
     make_table(z, other)
     own_lanes = pl.ds(pl.multiple_of(me_d * LANES, LANES), LANES)
 
@@ -443,16 +449,27 @@
                 acc[p] = acc[p] + product
 
     multiply(z, first=True)
+
+    def second_half(hop, found):
+        take_coef(found)
+        take_adj(hop)
+        table_loop(hop, other, len(found))
+        for _, zz in found:
+            multiply(zz)
+
+    before = []
     for hop in range(1, far + 1):
         shared = []
         for step in (-hop, hop) if hop < far else (hop,):
             copies.arrived(coef_sent[-step if hop < far else step], coef_block(chip(step), c), peer(step))
             shared.append(coef_share(chip(step)))
+        if hop == 4:
+            adj_take(4, 0)
         table_loop(hop, c, len(shared))
-        take_coef(shared)
-        table_loop(hop, other, len(shared))
-        for _, zz in shared:
-            multiply(zz)
+        if before:
+            second_half(hop - 1, before)
+        before = shared
+    second_half(far, before)
 
     low_rows, high_rows = acc.at[:, own : own + GHOST, :], acc.at[:, own + GHOST : ext, :]
     from_above = copies.start(low_rows, back.at[0], {"grp": below})

time: 72.2 us -> 66.9 us (0.927)
  Pallas kernels: 68.6 us -> 63.3 us
    pallas_call x1, Pallas kernels: 68.6 us -> 63.3 us  [local(): pl.pallas_call(functools.partial(kernel, (n_grp, n_dev, points, own, widt...]
where the time goes in v3:
time: 66.9 us; the launch traced here: 66.7 us
  Pallas kernels  63.3 us (95%)
  local copies, waits for them, and re-layouts  3.4 us (5%)
    pallas_call x1, Pallas kernels, local(): pl.pallas_call(functools.partial(kernel, (n_grp, n_dev, points, own, widt...  63.3 us
    unnamed x8, local copies, waits for them, and re-layouts  3.4 us

profile of v3, /device:TPU:1, one launch (start us, length us, event | category | flops | bytes accessed | tf_op | source)
XLA Modules:
  0.0 66.7 jit_solution(9132079687626596344)
XLA Ops:
  0.0 0.0 copy-start.2
  0.0 0.8 %copy.5.pat_ref = s32[128,24]{1,0:T(8,128)S(1)} copy(s32[128,24]{0,1:T(8,128)} %param.6) | data formatting | bytes 24576 | tf_op args[2]
  0.8 0.0 copy-done.2
  0.8 0.0 copy-start
  0.8 0.9 %copy-done = f32[2,128,256]{2,1,0:T(8,128)S(1)} copy-done((f32[2,128,256]{2,1,0:T(8,128)S(1)}, f32[2,128,256]{2,1,0:T(8,128)}, u32[]{:S(2)}) %copy-start) | copy-done | bytes 262168
  1.8 0.0 copy-start.1
  1.8 0.9 %copy-done.1 = bf16[2,128,384]{2,1,0:T(8,128)(2,1)S(1)} copy-done((bf16[2,128,384]{2,1,0:T(8,128)(2,1)S(1)}, bf16[2,128,384]{2,1,0:T(8,128)(2,1)}, u32[]{:S(2)}) %copy-start.1) | copy-done | bytes 196632
  2.7 63.3 %shard_map.46 = f32[2,128,256]{2,1,0:T(8,128)S(1)} custom-call(bf16[2,128,384]{2,1,0:T(8,128)(2,1)S(1)} %copy-done.1, f32[2,128,256]{2,1,0:T(8,128)S(1)} %copy-done, s32[128,24]{1,0:T(8,128)S(1)} %copy.5.pat_ref, s32[1,128]{1,0:T(1,128)S(1)} %bitcast.1), custom_call_target="tpu_custom_call" | custom-call | tf_op jit(solution)/shard_map/pallas_call | solution.py:495
  66.0 0.7 %copy.7 = f32[2,128,256]{2,1,0:T(8,128)} copy(f32[2,128,256]{2,1,0:T(8,128)S(1)} %shard_map.46) | data formatting | bytes 524288
Async XLA Ops:
  0.0 0.8 %copy-start.2 = (s32[128]{0:T(128)S(1)}, s32[128]{0:T(128)}, u32[]{:S(2)}) copy-start(s32[128]{0:T(128)} %param.7) | copy-start | bytes 1540
  0.8 1.0 %copy-start = (f32[2,128,256]{2,1,0:T(8,128)S(1)}, f32[2,128,256]{2,1,0:T(8,128)}, u32[]{:S(2)}) copy-start(f32[2,128,256]{2,1,0:T(8,128)} %adj_ref.1) | copy-start | bytes 786436
  1.8 0.9 %copy-start.1 = (bf16[2,128,384]{2,1,0:T(8,128)(2,1)S(1)}, bf16[2,128,384]{2,1,0:T(8,128)(2,1)}, u32[]{:S(2)}) copy-start(bf16[2,128,384]{2,1,0:T(8,128)(2,1)} %rows_ref.1) | copy-start | bytes 589828

commit v4 on v3

--- a/solution.py
+++ b/solution.py
@@ -357,7 +357,7 @@
             mat[slots, :, j0:slots, :] = mat[slots, :, j0:slots, :] - rhs * factors
             return carry
 
-        lax.fori_loop(0, 8, eliminate, 0)
+        lax.fori_loop(0, 8, eliminate, 0, unroll=True)
     at_slot = lax.broadcasted_iota(jnp.int32, (MEMBERS, slots, LANES), 1)
     solved = jnp.zeros((MEMBERS, slots, LANES), F32)
     for col in range(slots - 1, -1, -1):

time: 66.9 us -> 66.3 us (level)
  no operation moved by 1% of the time
where the time goes in v4:
time: 66.3 us; the launch traced here: 66.2 us
  Pallas kernels  62.7 us (95%)
  local copies, waits for them, and re-layouts  3.4 us (5%)
    pallas_call x1, Pallas kernels, local(): pl.pallas_call(functools.partial(kernel, (n_grp, n_dev, points, own, widt...  62.7 us
    unnamed x8, local copies, waits for them, and re-layouts  3.4 us

profile of v4, /device:TPU:1, one launch (start us, length us, event | category | flops | bytes accessed | tf_op | source)
XLA Modules:
  0.0 66.2 jit_solution(13414189081175234984)
XLA Ops:
  0.0 0.0 copy-start.2
  0.0 0.8 %copy.5.pat_ref = s32[128,24]{1,0:T(8,128)S(1)} copy(s32[128,24]{0,1:T(8,128)} %param.6) | data formatting | bytes 24576 | tf_op args[2]
  0.8 0.0 copy-done.2
  0.8 0.0 copy-start
  0.8 0.9 %copy-done = f32[2,128,256]{2,1,0:T(8,128)S(1)} copy-done((f32[2,128,256]{2,1,0:T(8,128)S(1)}, f32[2,128,256]{2,1,0:T(8,128)}, u32[]{:S(2)}) %copy-start) | copy-done | bytes 262168
  1.8 0.0 copy-start.1
  1.8 0.9 %copy-done.1 = bf16[2,128,384]{2,1,0:T(8,128)(2,1)S(1)} copy-done((bf16[2,128,384]{2,1,0:T(8,128)(2,1)S(1)}, bf16[2,128,384]{2,1,0:T(8,128)(2,1)}, u32[]{:S(2)}) %copy-start.1) | copy-done | bytes 196632
  2.7 62.7 %shard_map.46 = f32[2,128,256]{2,1,0:T(8,128)S(1)} custom-call(bf16[2,128,384]{2,1,0:T(8,128)(2,1)S(1)} %copy-done.1, f32[2,128,256]{2,1,0:T(8,128)S(1)} %copy-done, s32[128,24]{1,0:T(8,128)S(1)} %copy.5.pat_ref, s32[1,128]{1,0:T(1,128)S(1)} %bitcast.1), custom_call_target="tpu_custom_call" | custom-call | tf_op jit(solution)/shard_map/pallas_call | solution.py:495
  65.5 0.7 %copy.7 = f32[2,128,256]{2,1,0:T(8,128)} copy(f32[2,128,256]{2,1,0:T(8,128)S(1)} %shard_map.46) | data formatting | bytes 524288
Async XLA Ops:
  0.0 0.8 %copy-start.2 = (s32[128]{0:T(128)S(1)}, s32[128]{0:T(128)}, u32[]{:S(2)}) copy-start(s32[128]{0:T(128)} %param.7) | copy-start | bytes 1540
  0.8 1.0 %copy-start = (f32[2,128,256]{2,1,0:T(8,128)S(1)}, f32[2,128,256]{2,1,0:T(8,128)}, u32[]{:S(2)}) copy-start(f32[2,128,256]{2,1,0:T(8,128)} %adj_ref.1) | copy-start | bytes 786436
  1.8 0.9 %copy-start.1 = (bf16[2,128,384]{2,1,0:T(8,128)(2,1)S(1)}, bf16[2,128,384]{2,1,0:T(8,128)(2,1)}, u32[]{:S(2)}) copy-start(bf16[2,128,384]{2,1,0:T(8,128)(2,1)} %rows_ref.1) | copy-start | bytes 589828
